TPU v7x, 256 devices: a whole 4x4x8 slice. The times are simulated.
256 devices in a mesh: dp: 4 (over x), frame: 32 (over z, y), spatial: 2 (over core).
Axes of the slice: x: 4, y: 4, z: 8, core: 2. Of those that a mesh axis runs over, the one named last changes fastest.
Arguments:
- queries: bfloat16 [4, 32, 256, 3072], P('dp', 'frame', 'spatial'), may hold values from -120 to 120
- key_states: bfloat16 [4, 32, 256, 3072], P('dp', 'frame', 'spatial'), may hold values from -6 to 6
- value_states: bfloat16 [4, 32, 256, 3072], P('dp', 'frame', 'spatial'), may hold values from -6 to 6
- out_grad: bfloat16 [4, 32, 256, 3072], P('dp', 'frame', 'spatial'), may hold values from -6 to 6
- head_slopes: float32 [24], replicated, may hold values from 0.05 to 2
- timesteps: int32 [4, 32], P('dp', 'frame'), may hold values from 0 to 999
- stretch_frames: int32 [4, 32], P('dp', 'frame'), may hold values from 3 to 96, as said below
- valid_counts: int32 [4, 32], P('dp', 'frame'), may hold values from 64 to 256, as said below
- mod_weight: float32 [256, 3072], replicated, may hold values from -0.375 to 0.375
Outputs:
- query_grad: bfloat16 [4, 32, 256, 3072], P('dp', 'frame', 'spatial')
- key_grad: bfloat16 [4, 32, 256, 3072], P('dp', 'frame', 'spatial')
- value_grad: bfloat16 [4, 32, 256, 3072], P('dp', 'frame', 'spatial')
- mod_weight_grad: float32 [256, 3072], replicated
Inputs may be any that keep to these rules, and one draw needn't show every extreme that they name: `stretch_frames`: strictly increasing along each video's stretches, by 1 to 3 frames a stretch; each video's last stretch stands at frame 3 * 32. `valid_counts`: in every video some stretch is full.
All inputs are finite; a program needn't handle non-finite values.
Results may differ from a plain program's by a relative error of at most 0.02.
Values may be sent and summed in bfloat16 or wider, within the bound.
A program may use at most 128 MiB of HBM per device.

v0:
```python
import math

import jax
import jax.numpy as jnp
from jax import lax
from jax.experimental import pallas as pl
from jax.experimental.pallas import tpu as pltpu
from jax.sharding import PartitionSpec as P

MESH = pl.DeviceIdType.MESH
F32 = jnp.float32
BF16 = jnp.bfloat16
HIGHEST = lax.Precision.HIGHEST

NX, NZ, NY, NS = 4, 8, 4, 2
GROUP = NY * NS
SPAN = 3
SLOTS = SPAN + NY
TOK = 256
PART = TOK // NS
HEAD = 128
HEADS = 24
MINE = HEADS // GROUP
CHUNK = MINE * HEAD
WIDTH = HEADS * HEAD
FREQ = 256
SCALE = HEAD ** (-0.5)
LOG2E = math.log2(math.e)
HIDDEN = -1e30
NT = (((1,), (1,)), ((), ()))
TN = (((0,), (0,)), ((), ()))


def dot(a, b, dims=(((1,), (0,)), ((), ()))):
    return lax.dot_general(a, b, dims, preferred_element_type=F32)


def main_kernel(
    slope_ref, step_ref, frame_ref, count_ref, weight_ref,
    q_in, k_in, v_in, g_in,
    dq_out, dk_out, dv_out, mod_out,
    qb, kb, vb, gb, kt, vt, weight, meta, times, rows_t, gate, emb, emb_t, bias,
    x_s, p_s, d_s, dk_acc, dv_acc, dq_s, dk_s, dv_s, halo_s, halo_r, dgate, rows_y, terms,
    in_recv, in_send, z_recv, z_send, h_recv, h_send, o_recv, o_send,
    m_recv, m_send, t_recv, t_send, w_sem,
):
    x = lax.axis_index("dp")
    frame = lax.axis_index("frame")
    s = lax.axis_index("spatial")
    z = frame // NY
    y = frame % NY
    p = y * NS + s

    def group_dev(k):
        other = (p + k) % GROUP
        return (x, z * NY + other // NS, other % NS), other

    def y_dev(k):
        return (x, z * NY + (y + k) % NY, s)

    def z_dev(k):
        return (x, ((z + k) % NZ) * NY + y, s)

    def x_dev(k):
        return ((x + k) % NX, frame, s)

    def loop(low, high, body):
        def step(k, carry):
            body(k)
            return carry

        lax.fori_loop(low, high, step, 0)

    def send(src, dst, send_sem, recv_sem, device):
        pltpu.make_async_remote_copy(
            src_ref=src, dst_ref=dst, send_sem=send_sem, recv_sem=recv_sem,
            device_id=device, device_id_type=MESH,
        ).start()

    def wait(ref, sem):
        pltpu.make_async_copy(ref, ref, sem).wait()

    barrier = pltpu.get_barrier_semaphore()

    def greet(device):
        pl.semaphore_signal(barrier, inc=1, device_id=device, device_id_type=MESH)

    loop(1, GROUP, lambda k: greet(group_dev(k)[0]))
    loop(1, NZ, lambda k: greet(z_dev(k)))
    loop(1, NX, lambda k: greet(x_dev(k)))

    weight_copy = pltpu.make_async_copy(
        weight_ref.at[:, pl.ds(pl.multiple_of(p * CHUNK, HEAD), CHUNK)], weight, w_sem
    )
    weight_copy.start()
    line = lax.broadcasted_iota(jnp.int32, (8, HEAD), 0)
    steps = lax.broadcasted_iota(jnp.int32, (1, HEAD), 1).astype(F32)
    freq = jnp.exp(steps * (-math.log(10000.0) / (FREQ // 2)))
    meta[y] = jnp.where(
        line == 0, count_ref[0, 0], jnp.where(line == 1, frame_ref[0, 0], step_ref[0, 0])
    )
    arrays = ((k_in, kb, SPAN), (v_in, vb, SPAN), (q_in, qb, 0), (g_in, gb, 0))

    def column(owner, h):
        return pl.ds(pl.multiple_of(owner * CHUNK + h * HEAD, HEAD), HEAD)

    def own_part(a, h):
        src, dst, first = arrays[a]
        pltpu.make_async_copy(
            src.at[:, column(p, h)], dst.at[h, first + y, pl.ds(s * PART, PART)], in_recv.at[a, h]
        ).start()

    for a in range(4):
        loop(0, MINE, lambda h, a=a: own_part(a, h))

    pl.semaphore_wait(barrier, GROUP - 1 + NZ - 1 + NX - 1)

    loop(1, NY, lambda k: send(meta.at[y], meta.at[y], m_send.at[0], m_recv.at[0], y_dev(k)))

    def send_part(a, h, k):
        src, dst, first = arrays[a]
        device, owner = group_dev(k)
        send(
            src.at[:, column(owner, h)], dst.at[h, first + y, pl.ds(s * PART, PART)],
            in_send.at[a, h], in_recv.at[a, h], device,
        )

    def send_pair(first, h):
        for a in (first, first + 1):
            loop(1, GROUP, lambda k, a=a: send_part(a, h, k))

    send_pair(0, 0)
    send_pair(2, 0)
    send_pair(0, 1)

    wait(meta.at[pl.ds(0, NY - 1)], m_recv.at[0])
    times[x, z] = meta[...]
    loop(1, NZ, lambda k: send(meta, times.at[x, z], m_send.at[1], m_recv.at[1], z_dev(k)))
    rows_t[...] = jnp.zeros_like(rows_t)
    for i in range(NY):
        rows_t[i : i + 1, :] = meta[i, 2:3, :].astype(F32)
    angles = rows_t[0:8, :] * freq
    own_emb = jnp.concatenate([jnp.cos(angles), jnp.sin(angles)], axis=1)
    weight_copy.wait()
    gates = lax.dot_general(
        own_emb, weight[...], (((1,), (0,)), ((), ())), precision=HIGHEST, preferred_element_type=F32
    )
    for h in range(MINE):
        gate[h] = gates[:, h * HEAD : (h + 1) * HEAD]

    def pass_on(h):
        wait(kb.at[h, pl.ds(SPAN, NY)], in_recv.at[0, h])
        send(
            kb.at[h, pl.ds(NY, SPAN)], kb.at[h, pl.ds(0, SPAN)],
            z_send.at[0, h], z_recv.at[0, h], z_dev(1),
        )
        wait(vb.at[h, pl.ds(SPAN, NY)], in_recv.at[1, h])
        send(
            vb.at[h, pl.ds(NY, SPAN)], vb.at[h, pl.ds(0, SPAN)],
            z_send.at[1, h], z_recv.at[1, h], z_dev(1),
        )

    def arrive(h):
        wait(qb.at[h], in_recv.at[2, h])
        wait(gb.at[h], in_recv.at[3, h])

    pass_on(0)
    send_pair(0, 2)
    wait(times.at[0, pl.ds(0, NZ - 1)], m_recv.at[1])
    loop(1, NX, lambda k: send(times.at[x], times.at[x], m_send.at[2], m_recv.at[2], x_dev(k)))
    arrive(0)
    send_pair(2, 1)
    pass_on(1)
    send_pair(2, 2)

    wait(times.at[pl.ds(0, NX - 1)], m_recv.at[2])

    def take_row(n):
        for i in range(NY):
            rows_t[pl.ds(n * NY + i, 1), :] = times[n // NZ, n % NZ, i, 2:3, :].astype(F32)

    loop(0, NX * NZ, take_row)

    def features(n):
        angle = rows_t[pl.ds(pl.multiple_of(n * 8, 8), 8), :] * freq
        both = jnp.concatenate([jnp.cos(angle), jnp.sin(angle)], axis=1)
        for half in range(2):
            four = both[half * NY : (half + 1) * NY]
            tile = jnp.concatenate([four, four, four, four], axis=0)
            emb[pl.ds(pl.multiple_of(n * 32 + half * 16, 16), 16), :] = tile

    loop(0, NX * NZ // 2, features)
    emb_t[...] = emb[...].T.astype(BF16)

    token = lax.broadcasted_iota(jnp.int32, (TOK, HEAD), 0)
    z_before = (z + NZ - 1) % NZ
    has_before = jnp.minimum(z, 1)
    base = times[x, z, NY - 1, 1:2, :]

    def head(h):
        slope = slope_ref[p * MINE + h] * LOG2E
        for slot in range(SLOTS):
            if slot < SPAN:
                count = times[x, z_before, slot + 1, 0:1, :] * has_before
                place = times[x, z_before, slot + 1, 1:2, :]
            else:
                count = times[x, z, slot - SPAN, 0:1, :]
                place = times[x, z, slot - SPAN, 1:2, :]
            shift = (place - base).astype(F32) * slope
            bias[slot] = jnp.where(token < count, shift, HIDDEN)
        dk_acc[h] = jnp.zeros((SLOTS, TOK, HEAD), F32)
        dv_acc[h] = jnp.zeros((SLOTS, TOK, HEAD), F32)
        wait(kb.at[h, pl.ds(0, SPAN)], z_recv.at[0, h])
        wait(vb.at[h, pl.ds(0, SPAN)], z_recv.at[1, h])
        kt[...] = kb[h].reshape(SLOTS * TOK, HEAD).T
        vt[...] = vb[h].reshape(SLOTS * TOK, HEAD).T
        if h > 0:
            arrive(h)

        def stretch(i):
            q = qb[h, i]
            live = token < times[x, z, i, 0:1, :]
            grad = jnp.where(live, gb[h, i].astype(F32), 0.0)
            go = (gate[h, pl.ds(i, 1), :] * grad).astype(BF16)
            top = jnp.full((1, TOK), HIDDEN, F32)
            for k in range(SPAN + 1):
                one = bias[i + k]
                value = dot(kb[h, i + k], q, NT) * (SCALE * LOG2E) + jnp.concatenate([one, one], axis=1)
                x_s[k] = value
                top = jnp.maximum(top, jnp.max(value, axis=0, keepdims=True))
            total = jnp.zeros((1, TOK), F32)
            for k in range(SPAN + 1):
                value = jnp.exp2(x_s[k] - top)
                x_s[k] = value
                total = total + jnp.sum(value, axis=0, keepdims=True)
            inverse = 1.0 / total
            for k in range(SPAN + 1):
                value = x_s[k] * inverse
                x_s[k] = value
                p_s[k] = value.astype(BF16)
            window = pl.ds(pl.multiple_of(i * TOK, TOK), (SPAN + 1) * TOK)
            out_t = dot(vt[:, window], p_s[...].reshape((SPAN + 1) * TOK, TOK))
            delta = jnp.sum(go.astype(F32).T * out_t, axis=0, keepdims=True)
            dgate[h, pl.ds(y * NY + i, 1), :] = jnp.sum(grad * out_t.T, axis=0, keepdims=True)
            for k in range(SPAN + 1):
                d_s[k] = (x_s[k] * (dot(vb[h, i + k], go, NT) - delta) * SCALE).astype(BF16)
            dq_s[h, i] = dot(kt[:, window], d_s[...].reshape((SPAN + 1) * TOK, TOK)).T.astype(BF16)
            for k in range(SPAN + 1):
                dk_acc[h, i + k] += dot(d_s[k], q)
                dv_acc[h, i + k] += dot(p_s[k], go)

        loop(0, SPAN, stretch)
        halo_s[h, 0] = dk_acc[h, 0:SPAN].astype(BF16)
        halo_s[h, 1] = dv_acc[h, 0:SPAN].astype(BF16)
        send(halo_s.at[h], halo_r.at[h], h_send.at[h], h_recv.at[h], z_dev(NZ - 1))
        stretch(SPAN)

    def give_back(a, staged, out, h):
        def one(k):
            device, owner = group_dev(k)
            send(
                staged.at[h, owner // NS, pl.ds((owner % NS) * PART, PART)], out.at[:, column(p, h)],
                o_send.at[a], o_recv.at[a], device,
            )

        loop(1, GROUP, one)
        out[:, column(p, h)] = staged[h, y, pl.ds(pl.multiple_of(s * PART, PART), PART), :]

    has_after = jnp.minimum(NZ - 1 - z, 1).astype(F32)

    def finish(h):
        wait(halo_r.at[h], h_recv.at[h])
        for n, (acc, staged) in enumerate(((dk_acc, dk_s), (dv_acc, dv_s))):
            staged[h, 0] = acc[h, SPAN].astype(BF16)
            for i in range(1, NY):
                staged[h, i] = (
                    acc[h, SPAN + i] + halo_r[h, n, i - 1].astype(F32) * has_after
                ).astype(BF16)
        give_back(1, dk_s, dk_out, h)
        give_back(2, dv_s, dv_out, h)

    dgate[...] = jnp.zeros_like(dgate)
    def along_y(h):
        rows_y[h, y] = dgate[h].astype(BF16)
        mine = rows_y.at[h, y]
        loop(1, NY, lambda k: send(mine, mine, t_send.at[0, h], t_recv.at[0, h], y_dev(k)))

    def along_z(h):
        wait(rows_y.at[h, pl.ds(0, NY - 1)], t_recv.at[0, h])
        terms[h, s, x, z] = jnp.sum(rows_y[h].astype(F32), axis=0).astype(BF16)
        mine = terms.at[h, s, x, z]
        loop(1, NZ, lambda k: send(mine, mine, t_send.at[1, h], t_recv.at[1, h], z_dev(k)))

    def along_x(h):
        wait(terms.at[h, 0, 0, pl.ds(0, NZ - 1)], t_recv.at[1, h])
        mine = terms.at[h, s, x]
        loop(1, NX, lambda k: send(mine, mine, t_send.at[2, h], t_recv.at[2, h], x_dev(k)))

    def to_core(h):
        wait(terms.at[h, 0, pl.ds(0, NX - 1)], t_recv.at[2, h])
        send(terms.at[h, s], terms.at[h, s], t_send.at[3, h], t_recv.at[3, h], (x, frame, 1 - s))

    row = lax.broadcasted_iota(jnp.int32, (16, HEAD), 0)

    def contract(h):
        wait(terms.at[h, 0], t_recv.at[3, h])
        for other in range(NY):
            keep = jnp.where(row // NY == other, 1.0, 0.0).astype(BF16)
            cores = [(terms[h, core] * keep).reshape(NX * NZ * 16, HEAD) for core in range(NS)]
            both = jnp.concatenate(cores, axis=1)
            part = dot(emb_t[...], both)
            for core in range(NS):
                at = (other * NS + core) * CHUNK + h * HEAD
                mod_out[:, at : at + HEAD] = part[:, core * HEAD : (core + 1) * HEAD]

    head(0)
    along_y(0)
    give_back(0, dq_s, dq_out, 0)
    pass_on(2)
    head(1)
    along_y(1)
    give_back(0, dq_s, dq_out, 1)
    finish(0)
    along_z(0)
    head(2)
    along_y(2)
    along_x(0)
    along_z(1)
    give_back(0, dq_s, dq_out, 2)
    finish(1)
    along_x(1)
    to_core(0)
    along_z(2)
    finish(2)
    along_x(2)
    contract(0)
    to_core(1)
    to_core(2)
    contract(1)
    contract(2)

    outs = (dq_out, dk_out, dv_out)
    arrived = pl.ds(0, (GROUP - 1) * CHUNK)
    for a in range(3):
        wait(outs[a].at[:, arrived], o_recv.at[a])
        wait(outs[a].at[:, arrived], o_send.at[a])
    for a in range(4):
        for h in range(MINE):
            wait(q_in.at[:, pl.ds(0, (GROUP - 1) * HEAD)], in_send.at[a, h])
    for h in range(MINE):
        wait(kb.at[h, pl.ds(0, SPAN)], z_send.at[0, h])
        wait(vb.at[h, pl.ds(0, SPAN)], z_send.at[1, h])
        wait(halo_s.at[h], h_send.at[h])
    wait(meta.at[pl.ds(0, NY - 1)], m_send.at[0])
    wait(times.at[0, pl.ds(0, NZ - 1)], m_send.at[1])
    wait(times.at[pl.ds(0, NX - 1)], m_send.at[2])
    for h in range(MINE):
        wait(rows_y.at[h, pl.ds(0, NY - 1)], t_send.at[0, h])
        wait(terms.at[h, 0, 0, pl.ds(0, NZ - 1)], t_send.at[1, h])
        wait(terms.at[h, 0, pl.ds(0, NX - 1)], t_send.at[2, h])
        wait(terms.at[h, 0], t_send.at[3, h])


def store_kernel(dq, dk, dv, mod, dq_out, dk_out, dv_out, mod_out, sems):
    pairs = ((mod, mod_out), (dq, dq_out), (dk, dk_out), (dv, dv_out))
    copies = [pltpu.make_async_copy(src, dst, sems.at[n]) for n, (src, dst) in enumerate(pairs)]
    for copy in copies:
        copy.start()
    for copy in copies:
        copy.wait()


def in_vmem(array):
    return pltpu.with_memory_space_constraint(array, pltpu.VMEM)


def in_hbm(array):
    return pltpu.with_memory_space_constraint(array, pltpu.HBM)


def local(
    queries, key_states, value_states, out_grad, head_slopes, timesteps, stretch_frames,
    valid_counts, mod_weight,
):
    flat = (PART, WIDTH)
    anywhere = pl.BlockSpec(memory_space=pl.ANY)
    smem = pl.BlockSpec(memory_space=pltpu.SMEM)
    hbm = pl.BlockSpec(memory_space=pltpu.HBM)
    dma = pltpu.SemaphoreType.DMA
    grad = jax.ShapeDtypeStruct(flat, BF16)
    dq, dk, dv, mod = pl.pallas_call(
        main_kernel,
        name="attention_backward",
        out_shape=(pltpu.VMEM(flat, BF16),) * 3 + (pltpu.VMEM((FREQ, WIDTH), F32),),
        in_specs=[smem] * 4 + [hbm] * 5,
        out_specs=(pl.BlockSpec(memory_space=pltpu.VMEM),) * 4,
        scratch_shapes=[
            pltpu.VMEM((MINE, NY, TOK, HEAD), BF16),
            pltpu.VMEM((MINE, SLOTS, TOK, HEAD), BF16),
            pltpu.VMEM((MINE, SLOTS, TOK, HEAD), BF16),
            pltpu.VMEM((MINE, NY, TOK, HEAD), BF16),
            pltpu.VMEM((HEAD, SLOTS * TOK), BF16),
            pltpu.VMEM((HEAD, SLOTS * TOK), BF16),
            pltpu.VMEM((FREQ, CHUNK), F32),
            pltpu.VMEM((NY, 8, HEAD), jnp.int32),
            pltpu.VMEM((NX, NZ, NY, 8, HEAD), jnp.int32),
            pltpu.VMEM((NX * NZ * NY, HEAD), F32),
            pltpu.VMEM((MINE, 8, HEAD), F32),
            pltpu.VMEM((NX * NZ * 16, FREQ), F32),
            pltpu.VMEM((FREQ, NX * NZ * 16), BF16),
            pltpu.VMEM((SLOTS, TOK, HEAD), F32),
            pltpu.VMEM((SPAN + 1, TOK, TOK), F32),
            pltpu.VMEM((SPAN + 1, TOK, TOK), BF16),
            pltpu.VMEM((SPAN + 1, TOK, TOK), BF16),
            pltpu.VMEM((MINE, SLOTS, TOK, HEAD), F32),
            pltpu.VMEM((MINE, SLOTS, TOK, HEAD), F32),
            pltpu.VMEM((MINE, NY, TOK, HEAD), BF16),
            pltpu.VMEM((MINE, NY, TOK, HEAD), BF16),
            pltpu.VMEM((MINE, NY, TOK, HEAD), BF16),
            pltpu.VMEM((MINE, 2, SPAN, TOK, HEAD), BF16),
            pltpu.VMEM((MINE, 2, SPAN, TOK, HEAD), BF16),
            pltpu.VMEM((MINE, 16, HEAD), F32),
            pltpu.VMEM((MINE, NY, 16, HEAD), BF16),
            pltpu.VMEM((MINE, NS, NX, NZ, 16, HEAD), BF16),
            dma((4, MINE)), dma((4, MINE)),
            dma((2, MINE)), dma((2, MINE)),
            dma((MINE,)), dma((MINE,)),
            dma((3,)), dma((3,)),
            dma((3,)), dma((3,)),
            dma((4, MINE)), dma((4, MINE)),
            dma,
        ],
        compiler_params=pltpu.CompilerParams(
            collective_id=0, has_side_effects=True, vmem_limit_bytes=48 * 2**20
        ),
    )(
        in_hbm(head_slopes), timesteps, stretch_frames,
        valid_counts, in_hbm(mod_weight), in_hbm(queries.reshape(flat)),
        in_hbm(key_states.reshape(flat)), in_hbm(value_states.reshape(flat)),
        in_hbm(out_grad.reshape(flat)),
    )
    dq, dk, dv, mod = pl.pallas_call(
        store_kernel,
        name="store",
        out_shape=(pltpu.HBM(flat, BF16),) * 3 + (pltpu.HBM((FREQ, WIDTH), F32),),
        in_specs=[pl.BlockSpec(memory_space=pltpu.VMEM)] * 4,
        out_specs=(anywhere,) * 4,
        scratch_shapes=[dma((4,))],
        compiler_params=pltpu.CompilerParams(vmem_limit_bytes=4 * 2**20),
    )(in_vmem(dq), in_vmem(dk), in_vmem(dv), in_vmem(mod))
    whole = (1, 1, PART, WIDTH)
    return dq.reshape(whole), dk.reshape(whole), dv.reshape(whole), mod


def solution(mesh):
    tokens = P("dp", "frame", "spatial", None)
    each = P("dp", "frame")
    return jax.shard_map(
        local,
        mesh=mesh,
        in_specs=(tokens, tokens, tokens, tokens, P(), each, each, each, P()),
        out_specs=(tokens, tokens, tokens, P()),
        check_vma=False,
    )
```

profile of v0, /device:TPU:1, one launch (start us, length us, event | category | flops | bytes accessed | tf_op | source)
XLA Modules:
  0.0 85.5 jit_solution(5326382354029352274)
XLA Ops:
  2.6 80.5 %attention_backward.1 = (bf16[128,3072]{1,0:T(8,128)(2,1)S(1)}, bf16[128,3072]{1,0:T(8,128)(2,1)S(1)}, bf16[128,3072]{1,0:T(8,128)(2,1)S(1)}, f32[256,3072]{1,0:T(8,128)S(1)}) custom-call(f32[24]{0:T(128)} %slope_ref.1, s32[1,1]{1,0:T(1,128)S(6)} %copy.13.step_ref, s32[1,1]{1,0:T(1,128)S(6)} %copy.14.frame_ref, s32[1,1]{1,0:T(1,128)S(6)} %copy.15.count_ref, ...), custom_call_target="tpu_custom_call" | custom-call | tf_op jit(solution)/shard_map/attention_backward/pallas_call | solution.py:391
  83.1 2.5 %store.1 = (bf16[128,3072]{1,0:T(8,128)(2,1)}, bf16[128,3072]{1,0:T(8,128)(2,1)}, bf16[128,3072]{1,0:T(8,128)(2,1)}, f32[256,3072]{1,0:T(8,128)}) custom-call(bf16[128,3072]{1,0:T(8,128)(2,1)S(1)} %get-tuple-element.12.dq, bf16[128,3072]{1,0:T(8,128)(2,1)S(1)} %get-tuple-element.13.dk, bf16[128,3072]{1,0:T(8,128)(2,1)S(1)} %get-tuple-element.14.dv, ...), custom_call_target="tpu_custom_call" | custom-call | tf_op jit(solution)/shard_map/store/pallas_call | solution.py:442
where the time goes:
time: 85.7 us; the launch traced here: 85.5 us
  Pallas kernels  83 us (97%)
  between operations  2.58 us (3%)
    pallas_call x1, Pallas kernels, local(): pl.pallas_call(main_kernel, name='attention_backward', out_shape=(pltpu.V...  80.5 us
    pallas_call x1, Pallas kernels, local(): pl.pallas_call(store_kernel, name='store', out_shape=(pltpu.HBM(flat, BF1...  2.47 us

commit v1 on v0

--- a/solution.py
+++ b/solution.py
@@ -130,8 +130,8 @@
             loop(1, GROUP, lambda k, a=a: send_part(a, h, k))
 
     send_pair(0, 0)
+    send_pair(0, 1)
     send_pair(2, 0)
-    send_pair(0, 1)
 
     wait(meta.at[pl.ds(0, NY - 1)], m_recv.at[0])
     times[x, z] = meta[...]
@@ -168,9 +168,9 @@
     send_pair(0, 2)
     wait(times.at[0, pl.ds(0, NZ - 1)], m_recv.at[1])
     loop(1, NX, lambda k: send(times.at[x], times.at[x], m_send.at[2], m_recv.at[2], x_dev(k)))
+    pass_on(1)
+    send_pair(2, 1)
     arrive(0)
-    send_pair(2, 1)
-    pass_on(1)
     send_pair(2, 2)
 
     wait(times.at[pl.ds(0, NX - 1)], m_recv.at[2])

time: 85.7 us -> 85.7 us (level)
  no operation moved by 1% of the time
where the time goes in v1:
time: 85.7 us; the launch traced here: 85.6 us
  Pallas kernels  83 us (97%)
  between operations  2.58 us (3%)
    pallas_call x1, Pallas kernels, local(): pl.pallas_call(main_kernel, name='attention_backward', out_shape=(pltpu.V...  80.5 us
    pallas_call x1, Pallas kernels, local(): pl.pallas_call(store_kernel, name='store', out_shape=(pltpu.HBM(flat, BF1...  2.47 us

profile of v1, /device:TPU:1, one launch (start us, length us, event | category | flops | bytes accessed | tf_op | source)
XLA Modules:
  0.0 85.6 jit_solution(11088866486744922273)
XLA Ops:
  2.6 80.5 %attention_backward.1 = (bf16[128,3072]{1,0:T(8,128)(2,1)S(1)}, bf16[128,3072]{1,0:T(8,128)(2,1)S(1)}, bf16[128,3072]{1,0:T(8,128)(2,1)S(1)}, f32[256,3072]{1,0:T(8,128)S(1)}) custom-call(f32[24]{0:T(128)} %slope_ref.1, s32[1,1]{1,0:T(1,128)S(6)} %copy.13.step_ref, s32[1,1]{1,0:T(1,128)S(6)} %copy.14.frame_ref, s32[1,1]{1,0:T(1,128)S(6)} %copy.15.count_ref, ...), custom_call_target="tpu_custom_call" | custom-call | tf_op jit(solution)/shard_map/attention_backward/pallas_call | solution.py:391
  83.1 2.5 %store.1 = (bf16[128,3072]{1,0:T(8,128)(2,1)}, bf16[128,3072]{1,0:T(8,128)(2,1)}, bf16[128,3072]{1,0:T(8,128)(2,1)}, f32[256,3072]{1,0:T(8,128)}) custom-call(bf16[128,3072]{1,0:T(8,128)(2,1)S(1)} %get-tuple-element.12.dq, bf16[128,3072]{1,0:T(8,128)(2,1)S(1)} %get-tuple-element.13.dk, bf16[128,3072]{1,0:T(8,128)(2,1)S(1)} %get-tuple-element.14.dv, ...), custom_call_target="tpu_custom_call" | custom-call | tf_op jit(solution)/shard_map/store/pallas_call | solution.py:442

commit v2 on v0

--- a/solution.py
+++ b/solution.py
@@ -252,7 +252,10 @@
         loop(0, SPAN, stretch)
         halo_s[h, 0] = dk_acc[h, 0:SPAN].astype(BF16)
         halo_s[h, 1] = dv_acc[h, 0:SPAN].astype(BF16)
-        send(halo_s.at[h], halo_r.at[h], h_send.at[h], h_recv.at[h], z_dev(NZ - 1))
+        for n in range(2):
+            send(
+                halo_s.at[h, n], halo_r.at[h, n], h_send.at[n, h], h_recv.at[n, h], z_dev(NZ - 1)
+            )
         stretch(SPAN)
 
     def give_back(a, staged, out, h):
@@ -269,15 +272,14 @@
     has_after = jnp.minimum(NZ - 1 - z, 1).astype(F32)
 
     def finish(h):
-        wait(halo_r.at[h], h_recv.at[h])
-        for n, (acc, staged) in enumerate(((dk_acc, dk_s), (dv_acc, dv_s))):
+        for n, (acc, staged, out) in enumerate(((dk_acc, dk_s, dk_out), (dv_acc, dv_s, dv_out))):
+            wait(halo_r.at[h, n], h_recv.at[n, h])
             staged[h, 0] = acc[h, SPAN].astype(BF16)
             for i in range(1, NY):
                 staged[h, i] = (
                     acc[h, SPAN + i] + halo_r[h, n, i - 1].astype(F32) * has_after
                 ).astype(BF16)
-        give_back(1, dk_s, dk_out, h)
-        give_back(2, dv_s, dv_out, h)
+            give_back(1 + n, staged, out, h)
 
     dgate[...] = jnp.zeros_like(dgate)
     def along_y(h):
@@ -333,8 +335,8 @@
     along_z(2)
     finish(2)
     along_x(2)
+    to_core(1)
     contract(0)
-    to_core(1)
     to_core(2)
     contract(1)
     contract(2)
@@ -350,7 +352,8 @@
     for h in range(MINE):
         wait(kb.at[h, pl.ds(0, SPAN)], z_send.at[0, h])
         wait(vb.at[h, pl.ds(0, SPAN)], z_send.at[1, h])
-        wait(halo_s.at[h], h_send.at[h])
+        for n in range(2):
+            wait(halo_s.at[h, n], h_send.at[n, h])
     wait(meta.at[pl.ds(0, NY - 1)], m_send.at[0])
     wait(times.at[0, pl.ds(0, NZ - 1)], m_send.at[1])
     wait(times.at[pl.ds(0, NX - 1)], m_send.at[2])
@@ -424,7 +427,7 @@
             pltpu.VMEM((MINE, NS, NX, NZ, 16, HEAD), BF16),
             dma((4, MINE)), dma((4, MINE)),
             dma((2, MINE)), dma((2, MINE)),
-            dma((MINE,)), dma((MINE,)),
+            dma((2, MINE)), dma((2, MINE)),
             dma((3,)), dma((3,)),
             dma((3,)), dma((3,)),
             dma((4, MINE)), dma((4, MINE)),

time: 85.7 us -> 85.8 us (level)
  no operation moved by 1% of the time
where the time goes in v2:
time: 85.8 us; the launch traced here: 85.7 us
  Pallas kernels  83.1 us (97%)
  between operations  2.58 us (3%)
    pallas_call x1, Pallas kernels, local(): pl.pallas_call(main_kernel, name='attention_backward', out_shape=(pltpu.V...  80.6 us
    pallas_call x1, Pallas kernels, local(): pl.pallas_call(store_kernel, name='store', out_shape=(pltpu.HBM(flat, BF1...  2.47 us

profile of v2, /device:TPU:1, one launch (start us, length us, event | category | flops | bytes accessed | tf_op | source)
XLA Modules:
  0.0 85.7 jit_solution(11879981562614377679)
XLA Ops:
  2.6 80.6 %attention_backward.1 = (bf16[128,3072]{1,0:T(8,128)(2,1)S(1)}, bf16[128,3072]{1,0:T(8,128)(2,1)S(1)}, bf16[128,3072]{1,0:T(8,128)(2,1)S(1)}, f32[256,3072]{1,0:T(8,128)S(1)}) custom-call(f32[24]{0:T(128)} %slope_ref.1, s32[1,1]{1,0:T(1,128)S(6)} %copy.13.step_ref, s32[1,1]{1,0:T(1,128)S(6)} %copy.14.frame_ref, s32[1,1]{1,0:T(1,128)S(6)} %copy.15.count_ref, ...), custom_call_target="tpu_custom_call" | custom-call | tf_op jit(solution)/shard_map/attention_backward/pallas_call | solution.py:394
  83.2 2.5 %store.1 = (bf16[128,3072]{1,0:T(8,128)(2,1)}, bf16[128,3072]{1,0:T(8,128)(2,1)}, bf16[128,3072]{1,0:T(8,128)(2,1)}, f32[256,3072]{1,0:T(8,128)}) custom-call(bf16[128,3072]{1,0:T(8,128)(2,1)S(1)} %get-tuple-element.12.dq, bf16[128,3072]{1,0:T(8,128)(2,1)S(1)} %get-tuple-element.13.dk, bf16[128,3072]{1,0:T(8,128)(2,1)S(1)} %get-tuple-element.14.dv, ...), custom_call_target="tpu_custom_call" | custom-call | tf_op jit(solution)/shard_map/store/pallas_call | solution.py:445
